TPU v7x, 32 devices: a whole 2x2x4 slice. The times are simulated.
32 devices in a mesh: groups: 2 (over y), pages: 4 (over z), heads: 4 (over x, core).
Axes of the slice: x: 2, y: 2, z: 4, core: 2. Of those that a mesh axis runs over, the one named last changes fastest.
Arguments:
- q_nope: bfloat16 [256, 16384], P(('groups', 'pages'), 'heads'), parts along dimension 0, may hold values from -6 to 6
- q_rope: bfloat16 [256, 8192], P(('groups', 'pages'), 'heads'), parts along dimension 0, may hold values from -16 to 16
- cache_tiles: bfloat16 [12288, 576], P(('groups', 'pages')), parts along dimension 0, may hold values from -8 to 8
- absorb_keys: bfloat16 [128, 128, 512], P('heads'), may hold values from -0.5 to 0.5
- absorb_values: bfloat16 [128, 512, 128], P('heads'), may hold values from -2 to 2
- page_counts: int32 [8], P('groups'), parts along dimension 0, may hold values from 1 to 24, as said below
- query_token: int32 [256], P('groups'), parts along dimension 0, may hold values from 0 to 127, each once
- query_offsets: int32 [256], P('groups'), parts along dimension 0, may hold values from 512 to 2048
Outputs:
- attention_out: bfloat16 [256, 16384], P(('groups', 'pages'), 'heads'), parts along dimension 0
There are 2 independent parts, one for each index of `groups`. A program takes and returns all parts, laid end to end along the dimension named above; an argument that names none is the same for every part. Nothing has to cross between parts.
Inputs may be any that keep to these rules, and one draw needn't show every extreme that they name: Member m's live pages are its first page_counts[m] page slots; the counts sum to 32. `query_token`: a permutation of the span's tokens. Token t attends to the live cache rows whose key_position is below query_offsets[t].
All inputs are finite; a program needn't handle non-finite values.
Results may differ from a plain program's by a relative error of at most 0.022.
Values may be sent and summed in bfloat16 or wider, within the bound.
A program may use at most 64 MiB of HBM per device.

v0:
```python
import jax
import jax.numpy as jnp
from jax import lax
from jax.sharding import PartitionSpec as P

PAGE = 64
BLOCK_PAGES = 8


floor_score = -1e30


def on_device(
    q_nope, q_rope, cache_tiles, absorb_keys, absorb_values, page_counts, query_token, query_offsets
):
    member = lax.axis_index("pages")
    heads_here, nope_width, latent = absorb_keys.shape
    value_width = absorb_values.shape[2]
    local_rows = q_nope.shape[0]
    rope_width = q_rope.shape[1] // heads_here
    full_width = cache_tiles.shape[1]
    page_rows = PAGE
    slot_pages = cache_tiles.shape[0] // page_rows
    scale = (nope_width + rope_width) ** (-0.5)
    nope_local = q_nope.reshape(local_rows, heads_here, nope_width)
    rope_local = q_rope.reshape(local_rows, heads_here, rope_width)
    local_full = jnp.concatenate(
        [
            jnp.einsum(
                "qhn,hnl->qhl", nope_local, absorb_keys, preferred_element_type=jnp.float32
            ).astype(jnp.bfloat16),
            rope_local,
        ],
        axis=2,
    )
    gathered = lax.all_gather(local_full, "pages", axis=0, tiled=True)
    queries = gathered.shape[0]
    inverse = (
        jnp.zeros((queries,), jnp.int32).at[query_token].set(jnp.arange(queries, dtype=jnp.int32))
    )
    flat_queries = gathered[inverse].reshape(queries * heads_here, full_width)
    row_limits = jnp.repeat(query_offsets, heads_here)
    prefix = jnp.cumsum(page_counts) - page_counts
    pages_view = cache_tiles.reshape(slot_pages, page_rows, full_width)
    own_steps = jnp.arange(slot_pages, dtype=jnp.int32)
    logical = jnp.where(own_steps < page_counts[member], prefix[member] + own_steps, -1)
    live_pages = page_counts[member]
    block_pages = BLOCK_PAGES
    pool_pages = pages_view.shape[0]
    padded_length = -(-pool_pages // block_pages) * block_pages
    order_padded = jnp.concatenate([own_steps, jnp.zeros((padded_length - pool_pages,), jnp.int32)])
    block_count = (live_pages + block_pages - 1) // block_pages
    offsets_in_page = jnp.arange(page_rows, dtype=jnp.int32)
    far_away = jnp.int32(2**30)

    def attend(block, carry):
        running_max, running_sum, running_acc = carry
        chosen = lax.dynamic_slice_in_dim(order_padded, block * block_pages, block_pages)
        tiles = pages_view[chosen].reshape(block_pages * page_rows, full_width)
        usable = block * block_pages + jnp.arange(block_pages, dtype=jnp.int32) < live_pages
        positions = logical[chosen][:, None] * page_rows + offsets_in_page[None, :]
        positions = jnp.where(usable[:, None], positions, far_away).reshape(-1)
        scores = (
            lax.dot_general(
                flat_queries, tiles, (((1,), (1,)), ((), ())), preferred_element_type=jnp.float32
            )
            * scale
        )
        mask = positions[None, :] < row_limits[:, None]
        block_max = jnp.max(jnp.where(mask, scores, floor_score), axis=1)
        new_max = jnp.maximum(running_max, block_max)
        weights = jnp.where(mask, jnp.exp(scores - new_max[:, None]), 0.0)
        rescale = jnp.exp(running_max - new_max)
        new_sum = running_sum * rescale + jnp.sum(weights, axis=1)
        new_acc = running_acc * rescale[:, None] + jnp.dot(
            weights.astype(jnp.bfloat16), tiles[:, :latent], preferred_element_type=jnp.float32
        )
        return (new_max, new_sum, new_acc)

    rows_all = queries * heads_here
    initial = (
        jnp.full((rows_all,), floor_score, jnp.float32),
        jnp.zeros((rows_all,), jnp.float32),
        jnp.zeros((rows_all, latent), jnp.float32),
    )
    running_max, running_sum, running_acc = lax.fori_loop(0, block_count, attend, initial)
    local_max = running_max.reshape(queries, heads_here)
    global_max = lax.pmax(local_max, "pages")
    factor = jnp.exp(local_max - global_max)
    partial_den = running_sum.reshape(queries, heads_here) * factor
    partial_num = running_acc.reshape(queries, heads_here, latent) * factor[:, :, None]
    values_wide = absorb_values.astype(jnp.float32)
    projected = jnp.einsum(
        "qhl,hlv->qhv", partial_num, values_wide, precision=lax.Precision.HIGHEST
    )
    summed, totals = (
        lax.psum_scatter(
            projected.astype(jnp.bfloat16), "pages", scatter_dimension=0, tiled=True
        ).astype(jnp.float32),
        lax.psum_scatter(
            partial_den.astype(jnp.bfloat16), "pages", scatter_dimension=0, tiled=True
        ).astype(jnp.float32),
    )
    result = summed / totals[:, :, None]
    return result.reshape(local_rows, heads_here * value_width).astype(jnp.bfloat16)


def solution(mesh):
    in_specs = (
        P(("groups", "pages"), "heads"),
        P(("groups", "pages"), "heads"),
        P(("groups", "pages"), None),
        P("heads", None, None),
        P("heads", None, None),
        P("groups"),
        P("groups"),
        P("groups"),
    )
    out_specs = P(("groups", "pages"), "heads")
    return jax.shard_map(
        on_device, mesh=mesh, in_specs=in_specs, out_specs=out_specs, check_vma=False
    )
```

profile of v0, /device:TPU:0, one launch (start us, length us, event | category | flops | bytes accessed | tf_op | source)
XLA Modules:
  0.0 259.4 jit_solution(1545467615496081824)
XLA Ops:
  6.5 0.0 copy-start
  6.5 0.0 copy-start.3
  6.5 0.0 copy-start.4
  6.5 0.0 all-gather.2.cloned.1.call-start
  6.5 1.2 reshape.95
  7.8 0.1 copy.14
  7.9 0.0 copy-done
  7.9 2.9 %fusion.24 = bf16[32,32,512]{2,0,1:T(8,128)(2,1)S(1)} fusion(bf16[32,128,512]{2,1,0:T(8,128)(2,1)} %param.13, bf16[32,4096]{1,0:T(8,128)(2,1)S(1)} %copy-done), kind=kOutput, calls=%fused_computation.38 | convolution fusion | flops 134742016 | bytes 5505024 | tf_op jit(solution)/shard_map/qhn,hnl->qhl/dot_general | solution.py:29
  10.8 1.2 pad_maximum_fusion
  12.0 0.0 all-gather.2.cloned.1.call-update
  12.0 0.0 reduce-scatter.5.cloned.1.call-start
  12.1 0.0 copy-done.3
  12.1 0.6 dynamic_slice.10
  13.3 0.2 reduce-window.9
  13.5 0.6 dynamic_slice.11
  14.1 2.7 %copy.12 = bf16[1536,576]{1,0:T(8,128)(2,1)S(1)} copy(bf16[1536,576]{0,1:T(8,128)(2,1)} %param.12) | data formatting | bytes 3538944 | tf_op args[2]
  16.9 0.0 copy-done.4
  16.9 1.0 scatter_custom_fusion
  17.9 95.1 %all-gather.2.cloned.1.call-done = bf16[128,32,576]{2,0,1:T(8,128)(2,1)} async-done(((bf16[32,32,576]{2,0,1:T(8,128)(2,1)}), bf16[128,32,576]{2,0,1:T(8,128)(2,1)}) %all-gather.2.cloned.1.call-update) | async-done | bytes 4718608 | tf_op jit(solution)/shard_map/all_gather | solution.py:36
  113.0 7.8 %copy.15 = bf16[128,32,576]{2,1,0:T(8,128)(2,1)} copy(bf16[128,32,576]{2,0,1:T(8,128)(2,1)} %all-gather.2.cloned.1.call-done) | data formatting | bytes 9437184 | tf_op jit(solution)/shard_map/all_gather | solution.py:36
  120.8 0.0 copy-start.2
  120.8 6.0 %gather_fusion.2 = bf16[128,32,576]{2,1,0:T(8,128)(2,1)} fusion(bf16[128,32,576]{2,1,0:T(8,128)(2,1)} %copy.15, s32[1024]{0:T(1024)S(1)} %pad_clamp_fusion.1), kind=kCustom, calls=%fused_computation.2 | custom fusion | bytes 9437696 | tf_op jit(solution)/shard_map/gather | solution.py:41
  126.8 4.3 %broadcast_in_dim.54 = f32[4096,512]{1,0:T(8,128)} broadcast(f32[]{:T(128)} %constant.52.clone.1), dimensions={} | broadcast | bytes 8388612 | tf_op jit(solution)/shard_map/broadcast_in_dim | solution.py:84
  131.1 0.0 copy-done.2
  131.1 19.0 %while.16 = (s32[]{:T(128)}, f32[4096]{0:T(1024)S(1)}, f32[4096]{0:T(1024)S(1)}, f32[4096,512]{1,0:T(8,128)}, s32[]{:T(128)}, /*index=5*/s32[]{:T(128)}, s32[24]...) while((s32[]{:T(128)}, f32[4096]{0:T(1024)S(1)}, ...), condition=%wide.region_5.6_spmd.clone.clone, body=%wide.region_2.5_spmd.clone.clone.sunk | while | flops 4596967424 | bytes 108053704 | solution.py:86
  131.1 0.1 compare_select_fusion.9
  131.2 0.6 add_compare_fusion.2
  131.8 1.2 compare_select_fusion.8
  133.1 0.6 gather_fusion
  133.7 0.1 fusion.47
  133.8 0.1 select_n.96
  133.9 0.1 broadcast_in_dim.99
  134.0 0.1 lt.144
  134.0 0.7 gather_fusion.1
  134.7 0.0 slice-start
  134.7 0.0 slice-start.1
  134.7 5.8 %fusion.48 = (f32[4096]{0:T(1024)S(1)}, f32[512,4096]{1,0:T(8,128)S(1)}) fusion(s32[4096]{0:T(1024)S(1)} %lt.144, s32[512]{0:T(512)S(1)} %select_n.96, bf16[512,576]{1,0:T(8,128)(2,1)S(1)} %bitcast.57, bf16[4096,576]{1,0:T(8,128)(2,1)} %get-tuple-element.276), kind=kOutput, calls=%fused_computation.9.clone.1 | convolution fusion | flops 2424303616 | bytes 13731840 | tf_op jit(solution)/shard_map/while/body/dot_general | solution.py:64
  140.5 2.2 fusion.49
  142.7 0.0 slice-done
  142.8 0.0 slice-done.1
  142.8 4.1 %multiply_add_fusion.5 = f32[4096,512]{1,0:T(8,128)S(1)} fusion(f32[4096,512]{1,0:T(8,128)S(1)} %bitcast.55, f32[512,4096]{1,0:T(8,128)S(1)} %get-tuple-element.235, f32[4096]{0:T(1024)S(1)} %get-tuple-element.237, f32[4096]{0:T(1024)S(1)} %max.8, s32[4096]{0:T(1024)S(1)} %lt.144, s32[512]{0:T(512)S(1)} %select_n.96, bf16[512,576]{1,0:T(8,128)(2,1)S(1)} %bitcast.58), kind=kOutput, calls=%fused_computation.12.clone.1 | convolution fusion | flops 2162163712 | bytes 25741312 | tf_op jit(solution)/shard_map/while/body/dot_general | solution.py:75
  146.9 0.0 copy-start.1
  146.9 3.2 %copy-done.1 = f32[4096,512]{1,0:T(8,128)} copy-done((f32[4096,512]{1,0:T(8,128)}, f32[4096,512]{1,0:T(8,128)S(1)}, u32[]{:S(2)}) %copy-start.1) | copy-done | bytes 8388632 | tf_op jit(solution)/shard_map/while
  150.1 0.1 reshape.98
  150.2 54.8 %pmax.7 = f32[128,32]{1,0:T(8,128)S(1)} all-reduce(f32[128,32]{1,0:T(8,128)S(1)} %reshape.98), channel_id=1, replica_groups=mesh['groups'=2,'pages'=4,'heads'=4] {'pages'}, use_global_device_ids=true, to_apply=%region_6.7 | all-reduce | flops 4096 | bytes 32768 | tf_op jit(solution)/shard_map/pmax | solution.py:88
  205.0 0.1 reshape.99
  205.1 0.6 multiply_convert_fusion
  205.8 0.0 reduce-scatter.5.cloned.1.call-update
  205.8 0.3 reduce-scatter.3.cloned.1.call-start
  206.0 0.1 copy.16
  206.1 13.8 %fusion.23 = bf16[128,32,128]{2,0,1:T(8,128)(2,1)} fusion(bf16[32,512,128]{2,1,0:T(8,128)(2,1)} %param.14, f32[128,32,512]{2,1,0:T(8,128)} %bitcast.56, f32[128,32]{0,1:T(8,128)S(1)} %copy.16), kind=kOutput, calls=%fused_computation.37 | convolution fusion | flops 3223846912 | bytes 13647872 | tf_op jit(solution)/shard_map/qhl,hlv->qhv/dot_general | solution.py:93
  219.9 0.0 reduce-scatter.3.cloned.1.call-update
  219.9 3.4 %reduce-scatter.5.cloned.1.call-done = bf16[32,32]{1,0:T(8,128)(2,1)} async-done(((bf16[128,32]{1,0:T(8,128)(2,1)}), bf16[32,32]{1,0:T(8,128)(2,1)}) %reduce-scatter.5.cloned.1.call-update) | async-done | bytes 2064 | tf_op jit(solution)/shard_map/reduce_scatter | solution.py:100
  223.3 0.8 copy.18
  224.0 27.0 %reduce-scatter.3.cloned.1.call-done = bf16[32,32,128]{2,0,1:T(8,128)(2,1)} async-done(((bf16[128,32,128]{2,0,1:T(8,128)(2,1)}), bf16[32,32,128]{2,0,1:T(8,128)(2,1)}) %reduce-scatter.3.cloned.1.call-update) | async-done | bytes 262160 | tf_op jit(solution)/shard_map/reduce_scatter | solution.py:97
  251.0 1.9 copy_bitcast_fusion
  (14 shorter events, 0.1 us)
Async XLA Ops:
  6.5 1.3 copy-start
  6.5 5.5 %copy-start.3 = (s32[4]{0:T(128)S(1)}, s32[4]{0:T(128)}, u32[]{:S(2)}) copy-start(s32[4]{0:T(128)} %param.15) | copy-start | bytes 52
  6.5 10.4 %copy-start.4 = (s32[128]{0:T(128)S(1)}, s32[128]{0:T(128)}, u32[]{:S(2)}) copy-start(s32[128]{0:T(128)} %param.16) | copy-start | bytes 1540
  6.5 106.5 %all-gather.2.cloned.1.call-start = ((), (), s32[]{:S(2)}) async-start(), calls=%async_computation.2 | async-start | bytes 6553600 | tf_op jit(solution)/shard_map/all_gather | solution.py:36
  12.0 211.2 %reduce-scatter.5.cloned.1.call-start = ((), (), s32[]{:S(2)}) async-start(), calls=%async_computation.4 | async-start | bytes 40960 | tf_op jit(solution)/shard_map/reduce_scatter | solution.py:100
  120.8 10.3 %copy-start.2 = (s32[128]{0:T(128)S(1)}, s32[128]{0:T(128)}, u32[]{:S(2)}) copy-start(s32[128]{0:T(128)} %param.17) | copy-start | bytes 1540
  134.7 8.0 %slice-start = ((s8[8388608]{0:T(1024)(128)(4,1)}), s8[4194304]{0:T(1024)(128)(4,1)S(1)}, s32[]{:S(2)}) async-start(s8[8388608]{0:T(1024)(128)(4,1)} %bitcast.54), calls=%async_computation.5 | async-start | bytes 8388608 | tf_op jit(solution)/shard_map/while
  134.7 8.0 %slice-start.1 = ((s8[8388608]{0:T(1024)(128)(4,1)}), s8[4194304]{0:T(1024)(128)(4,1)S(1)}, s32[]{:S(2)}) async-start(s8[8388608]{0:T(1024)(128)(4,1)} %bitcast.54), calls=%async_computation.6 | async-start | bytes 8388608 | tf_op jit(solution)/shard_map/while
  146.9 3.2 %copy-start.1 = (f32[4096,512]{1,0:T(8,128)}, f32[4096,512]{1,0:T(8,128)S(1)}, u32[]{:S(2)}) copy-start(f32[4096,512]{1,0:T(8,128)S(1)} %multiply_add_fusion.5) | copy-start | bytes 25165828 | tf_op jit(solution)/shard_map/while
  205.8 45.2 %reduce-scatter.3.cloned.1.call-start = ((), (), s32[]{:S(2)}) async-start(), calls=%async_computation.3 | async-start | bytes 1310720 | tf_op jit(solution)/shard_map/reduce_scatter | solution.py:97
Sparse Core Ops, SparseCore 0:
  12.2 100.8 all-gather.1
  205.9 17.3 reduce-scatter.4
  225.7 25.2 reduce-scatter.2
where the time goes:
time: 259 us
  waiting for transfers between devices  125 us (48%)
  blocking collectives  54.8 us (21%)
  local copies, waits for them, and re-layouts  30.1 us (12%)
  matrix products  26.5 us (10%)
  between operations  13.9 us (5%)
  other arithmetic  8.18 us (3%)
    all_gather x1, waiting for transfers between devices, on_device(): gathered = lax.all_gather(local_full, 'pages', axis=0, tiled=True)  95.1 us
    pmax x1, blocking collectives, on_device(): global_max = lax.pmax(local_max, 'pages')  54.8 us
    reduce_scatter x1, waiting for transfers between devices, on_device(): lax.psum_scatter(projected.astype(jnp.bfloat16), 'pages', scatter_dimensi...  27 us
    dot_general x1, matrix products, on_device(): jnp.einsum('qhl,hlv->qhv', partial_num, values_wide, precision=lax.Precis...  13.8 us
    all_gather x1, local copies, waits for them, and re-layouts, on_device(): gathered = lax.all_gather(local_full, 'pages', axis=0, tiled=True)  7.78 us
    gather x1, local copies, waits for them, and re-layouts, on_device(): flat_queries = gathered[inverse].reshape(queries * heads_here, full_width)  6.02 us
    dot_general x1, matrix products, attend(): lax.dot_general(flat_queries, tiles, (((1,), (1,)), ((), ())), preferred_...  5.76 us
  transfers between devices with their start and end apart: 3, of which 3 were waited for; matrix products, arithmetic and copies ran while one was open for 8% of the time, Pallas kernels for 0%

commit v1 on v0

v1 whole, which is shorter than its diff:
```python
import functools
import math

import jax
import jax.numpy as jnp
from jax import lax
from jax.experimental import pallas as pl
from jax.experimental.pallas import tpu as pltpu
from jax.sharding import PartitionSpec as P

PAGE = 64
SLOTS_PER_LIVE = 3
HEAD_BLOCK = 8
NEG = -1e30


def attend_kernel(factor, limits_ref, nope_ref, rope_ref, keys_ref, wk_ref, wv_ref, out_ref):
    block, nope_width, latent = wk_ref.shape
    rows = nope_ref.shape[0]
    value_width = wv_ref.shape[2]
    rope_width = rope_ref.shape[1] // block
    latents = []
    ropes = []
    for h in range(block):
        latents.append(
            jnp.dot(
                nope_ref[:, h * nope_width : (h + 1) * nope_width],
                wk_ref[h],
                preferred_element_type=jnp.float32,
            ).astype(jnp.bfloat16)
        )
        ropes.append(rope_ref[:, h * rope_width : (h + 1) * rope_width])
    q_latent = jnp.concatenate(latents, axis=0)
    q_rope = jnp.concatenate(ropes, axis=0)
    contract = (((1,), (1,)), ((), ()))
    scores = lax.dot_general(
        q_latent, keys_ref[:, :latent], contract, preferred_element_type=jnp.float32
    ) + lax.dot_general(
        q_rope, keys_ref[:, latent:], contract, preferred_element_type=jnp.float32
    )
    limits = jnp.concatenate([limits_ref[...]] * block, axis=0)
    position = lax.broadcasted_iota(jnp.int32, scores.shape, 1)
    scores = jnp.where(position < limits, scores, NEG)
    top = jnp.max(scores, axis=1, keepdims=True)
    weights = jnp.exp2((scores - top) * factor)
    total = jnp.sum(weights, axis=1, keepdims=True)
    mixed = jnp.dot(
        weights.astype(jnp.bfloat16), keys_ref[:, :latent], preferred_element_type=jnp.float32
    )
    mixed = (mixed / total).astype(jnp.bfloat16)
    for h in range(block):
        out_ref[:, h * value_width : (h + 1) * value_width] = jnp.dot(
            mixed[h * rows : (h + 1) * rows], wv_ref[h], preferred_element_type=jnp.float32
        ).astype(out_ref.dtype)


def attend(limits, q_nope, q_rope, keys, absorb_keys, absorb_values):
    heads, nope_width, latent = absorb_keys.shape
    value_width = absorb_values.shape[2]
    rows = q_nope.shape[0]
    rope_width = q_rope.shape[1] // heads
    block = min(HEAD_BLOCK, heads)
    factor = (nope_width + rope_width) ** (-0.5) * math.log2(math.e)
    live, full = keys.shape
    return pl.pallas_call(
        functools.partial(attend_kernel, factor),
        grid=(heads // block,),
        out_shape=jax.ShapeDtypeStruct((rows, heads * value_width), jnp.bfloat16),
        in_specs=[
            pl.BlockSpec((rows, 1), lambda i: (0, 0)),
            pl.BlockSpec((rows, block * nope_width), lambda i: (0, i)),
            pl.BlockSpec((rows, block * rope_width), lambda i: (0, i)),
            pl.BlockSpec((live, full), lambda i: (0, 0)),
            pl.BlockSpec((block, nope_width, latent), lambda i: (i, 0, 0)),
            pl.BlockSpec((block, latent, value_width), lambda i: (i, 0, 0)),
        ],
        out_specs=pl.BlockSpec((rows, block * value_width), lambda i: (0, i)),
        compiler_params=pltpu.CompilerParams(vmem_limit_bytes=56 * 2**20),
        cost_estimate=pl.CostEstimate(
            flops=2 * rows * heads * live * (full + latent),
            bytes_accessed=2 * (absorb_keys.size + absorb_values.size + keys.size),
            transcendentals=rows * heads * live,
        ),
    )(limits, q_nope, q_rope, keys, absorb_keys, absorb_values)


def own_part(cache_tiles, page_counts, members, parts):
    member = lax.axis_index("pages")
    part = lax.axis_index("heads")
    slot_rows, full = cache_tiles.shape
    live_rows = slot_rows * members // SLOTS_PER_LIVE
    length = live_rows // parts
    before = jnp.sum(jnp.where(jnp.arange(members) < member, page_counts, 0)) * PAGE
    count = jnp.sum(jnp.where(jnp.arange(members) == member, page_counts, 0)) * PAGE
    start = jnp.clip(part * length - before, -length, slot_rows)
    padded = jnp.pad(cache_tiles, ((length, length), (0, 0)))
    rows = lax.dynamic_slice(padded, (start + length, 0), (length, full))
    index = start + jnp.arange(length)
    mine = (index >= 0) & (index < count)
    return jnp.where(mine[:, None], rows, jnp.zeros((), rows.dtype))


def on_device(
    members,
    parts,
    q_nope,
    q_rope,
    cache_tiles,
    absorb_keys,
    absorb_values,
    page_counts,
    query_token,
    query_offsets,
):
    member = lax.axis_index("pages")
    rows = q_nope.shape[0]
    tokens = query_token.shape[0]
    own = own_part(cache_tiles, page_counts, members, parts)
    merged = lax.psum(own, "pages")
    keys = lax.all_gather(merged, "heads", axis=0, tiled=True)
    my_token = lax.dynamic_slice(query_token, (member * rows,), (rows,))
    limits = jnp.sum(
        jnp.where(my_token[:, None] == jnp.arange(tokens)[None, :], query_offsets[None, :], 0),
        axis=1,
        keepdims=True,
    )
    out = attend(limits, q_nope, q_rope, keys, absorb_keys, absorb_values)
    gathered = lax.all_gather(out, "pages", axis=0, tiled=True)
    wanted = member * rows + jnp.arange(rows)
    pick = (wanted[:, None] == query_token[None, :]).astype(jnp.bfloat16)
    return jnp.dot(pick, gathered, preferred_element_type=jnp.float32).astype(jnp.bfloat16)


def solution(mesh):
    in_specs = (
        P(("groups", "pages"), "heads"),
        P(("groups", "pages"), "heads"),
        P(("groups", "pages"), None),
        P("heads", None, None),
        P("heads", None, None),
        P("groups"),
        P("groups"),
        P("groups"),
    )
    out_specs = P(("groups", "pages"), "heads")
    return jax.shard_map(
        functools.partial(on_device, mesh.shape["pages"], mesh.shape["heads"]),
        mesh=mesh,
        in_specs=in_specs,
        out_specs=out_specs,
        check_vma=False,
    )
```

time: 259 us -> 133 us (0.51)
  blocking collectives: 54.8 us -> 0 us
  waiting for transfers between devices: 125 us -> 97 us
  local copies, waits for them, and re-layouts: 30.1 us -> 3.52 us
  matrix products: 26.5 us -> 2.25 us
  Pallas kernels: 0 us -> 12.4 us
  other arithmetic: 8.18 us -> 2.63 us
    pmax x1 -> x0, blocking collectives: 54.8 us -> none  [on_device(): global_max = lax.pmax(local_max, 'pages')]
    psum x0 -> x1, waiting for transfers between devices: none -> 43.3 us  [on_device(): merged = lax.psum(own, 'pages')]
    all_gather x1 -> x2, waiting for transfers between devices: 95.1 us -> 53.7 us  [the longest x1 28.1 us: on_device(): gathered = lax.all_gather(out, 'pages', axis=0, tiled=True)]
    reduce_scatter x2 -> x0, waiting for transfers between devices: 30.3 us -> none  [the longest x1 27 us: on_device(): lax.psum_scatter(projected.astype(jnp.bfloat16), 'pages', scatter_dimensi...]
    dot_general x4 -> x1, matrix products: 26.5 us -> 2.25 us  [on_device(): jnp.dot(pick, gathered, preferred_element_type=jnp.float32)]
    pallas_call x0 -> x1, Pallas kernels: none -> 12.4 us  [attend(): pl.pallas_call(functools.partial(attend_kernel, factor), grid=(heads // b...]
    all_gather x1 -> x0, local copies, waits for them, and re-layouts: 7.78 us -> none  [on_device(): gathered = lax.all_gather(local_full, 'pages', axis=0, tiled=True)]
    gather x3 -> x0, local copies, waits for them, and re-layouts: 7.34 us -> none  [the longest x1 6.02 us: on_device(): flat_queries = gathered[inverse].reshape(queries * heads_here, full_width)]
  transfers between devices with their start and end apart: 3 -> 3, of which waited for: 3 -> 3; matrix products, arithmetic and copies ran while one was open for 8% -> 1% of each run, Pallas kernels for 0% -> 0%
where the time goes in v1:
time: 133 us; the launch traced here: 132 us
  waiting for transfers between devices  97 us (73%)
  between operations  14.4 us (11%)
  Pallas kernels  12.4 us (9%)
  local copies, waits for them, and re-layouts  3.52 us (3%)
  other arithmetic  2.63 us (2%)
  matrix products  2.25 us (2%)
    psum x1, waiting for transfers between devices, on_device(): merged = lax.psum(own, 'pages')  43.3 us
    all_gather x1, waiting for transfers between devices, on_device(): gathered = lax.all_gather(out, 'pages', axis=0, tiled=True)  28.1 us
    all_gather x1, waiting for transfers between devices, on_device(): keys = lax.all_gather(merged, 'heads', axis=0, tiled=True)  25.6 us
    pallas_call x1, Pallas kernels, attend(): pl.pallas_call(functools.partial(attend_kernel, factor), grid=(heads // b...  12.4 us
    unnamed x5, local copies, waits for them, and re-layouts  2.75 us
  transfers between devices with their start and end apart: 3, of which 3 were waited for; matrix products, arithmetic and copies ran while one was open for 1% of the time, Pallas kernels for 0%

profile of v1, /device:TPU:0, one launch (start us, length us, event | category | flops | bytes accessed | tf_op | source)
XLA Modules:
  0.0 132.3 jit_solution(11877252146117549926)
XLA Ops:
  6.5 0.0 all-reduce.3.cloned.1.call-start
  6.5 1.3 fusion.8
  9.1 2.7 %copy.11 = bf16[1536,576]{1,0:T(8,128)(2,1)S(1)} copy(bf16[1536,576]{0,1:T(8,128)(2,1)} %param.10) | data formatting | bytes 3538944 | tf_op args[2]
  11.8 0.0 copy-start
  11.8 0.0 copy-start.1
  11.8 1.2 fusion
  13.0 0.0 all-reduce.3.cloned.1.call-update
  13.0 0.0 all-gather.3.cloned.1.call-start
  13.1 43.3 %all-reduce.3.cloned.1.call-done = bf16[512,576]{1,0:T(8,128)(2,1)} async-done(((bf16[512,576]{1,0:T(8,128)(2,1)}), bf16[512,576]{1,0:T(8,128)(2,1)}) %all-reduce.3.cloned.1.call-update) | async-done | bytes 589840 | tf_op jit(solution)/shard_map/psum | solution.py:119
  56.4 0.0 all-gather.3.cloned.1.call-update
  56.4 0.0 all-gather.5.cloned.1.call-start
  56.4 0.0 copy-done
  56.5 0.1 dynamic_slice.6
  56.5 0.0 copy-done.1
  56.5 0.2 select_reduce_fusion
  56.7 0.7 copy.12.limits_ref
  57.4 25.6 %all-gather.3.cloned.1.call-done.keys_ref = bf16[2048,576]{1,0:T(8,128)(2,1)} async-done(((bf16[512,576]{1,0:T(8,128)(2,1)}), bf16[2048,576]{1,0:T(8,128)(2,1)}) %all-gather.3.cloned.1.call-update) | async-done | bytes 2359312 | tf_op jit(solution)/shard_map/all_gather | solution.py:120
  83.0 12.4 %shard_map.82 = bf16[32,4096]{1,0:T(8,128)(2,1)} custom-call(s32[32,1]{1,0:T(8,128)} %copy.12.limits_ref, bf16[32,4096]{1,0:T(8,128)(2,1)} %nope_ref.1, bf16[32,2048]{1,0:T(8,128)(2,1)} %rope_ref.1, bf16[2048,576]{1,0:T(8,128)(2,1)} %all-gather.3.cloned.1.call-done.keys_ref, bf16[32,128,512]{2,1,0:T(8,128)(2,1)} %wk_ref.1, bf16[32,512,128]{2,1,0:T(8,128)(2,1)} %wv_ref.1), custom_call_target="tpu_custom_call" | custom-call | flops 4563402752 | bytes 10747904 | tf_op jit(solution)/shard_map/pallas_call | solution.py:65
  95.4 0.0 all-gather.5.cloned.1.call-update
  95.4 28.1 %all-gather.5.cloned.1.call-done = bf16[128,4096]{1,0:T(8,128)(2,1)} async-done(((bf16[32,4096]{1,0:T(8,128)(2,1)}), bf16[128,4096]{1,0:T(8,128)(2,1)}) %all-gather.5.cloned.1.call-update) | async-done | bytes 1048592 | tf_op jit(solution)/shard_map/all_gather | solution.py:128
  123.5 2.2 %convolution_convert_fusion = bf16[32,4096]{1,0:T(8,128)(2,1)} fusion(bf16[128,4096]{1,0:T(8,128)(2,1)} %all-gather.5.cloned.1.call-done, s32[128]{0:T(128)S(1)} %copy-done, s32[32]{0:T(128)S(1)} %iota_add_fusion.1), kind=kOutput, calls=%fused_computation | convolution fusion | flops 33689600 | bytes 1311360 | tf_op jit(solution)/shard_map/dot_general | solution.py:131
  (2 shorter events, 0.0 us)
Async XLA Ops:
  6.5 49.8 %all-reduce.3.cloned.1.call-start = ((), (), s32[]{:S(2)}) async-start(), calls=%async_computation | async-start | bytes 1310720 | tf_op jit(solution)/shard_map/psum | solution.py:119
  11.8 44.6 %copy-start = (s32[128]{0:T(128)S(1)}, s32[128]{0:T(128)}, u32[]{:S(2)}) copy-start(s32[128]{0:T(128)} %param.14) | copy-start | bytes 1540
  11.8 44.7 %copy-start.1 = (s32[128]{0:T(128)S(1)}, s32[128]{0:T(128)}, u32[]{:S(2)}) copy-start(s32[128]{0:T(128)} %param.15) | copy-start | bytes 1540
  13.0 70.0 %all-gather.3.cloned.1.call-start = ((), (), s32[]{:S(2)}) async-start(), calls=%async_computation.1 | async-start | bytes 3276800 | tf_op jit(solution)/shard_map/all_gather | solution.py:120
  56.4 67.1 %all-gather.5.cloned.1.call-start = ((), (), s32[]{:S(2)}) async-start(), calls=%async_computation.2 | async-start | bytes 1310720 | tf_op jit(solution)/shard_map/all_gather | solution.py:128
Sparse Core Ops, SparseCore 0:
  13.1 43.1 all-reduce.2
  57.9 25.0 all-gather.2
  95.5 27.9 all-gather.4

commit v2 on v1

--- a/solution.py
+++ b/solution.py
@@ -11,6 +11,8 @@
 PAGE = 64
 SLOTS_PER_LIVE = 3
 HEAD_BLOCK = 8
+CORES = 2
+MESH = pl.DeviceIdType.MESH
 NEG = -1e30
 
 
@@ -84,20 +86,196 @@
     )(limits, q_nope, q_rope, keys, absorb_keys, absorb_values)
 
 
+def page_kernel(place_ref, cache_ref, out_ref):
+    slot = place_ref[0] + pl.program_id(0)
+    live = (slot >= 0) & (slot < place_ref[1])
+    out_ref[...] = jnp.where(live, cache_ref[...], jnp.zeros_like(cache_ref))
+
+
 def own_part(cache_tiles, page_counts, members, parts):
     member = lax.axis_index("pages")
     part = lax.axis_index("heads")
     slot_rows, full = cache_tiles.shape
-    live_rows = slot_rows * members // SLOTS_PER_LIVE
-    length = live_rows // parts
-    before = jnp.sum(jnp.where(jnp.arange(members) < member, page_counts, 0)) * PAGE
-    count = jnp.sum(jnp.where(jnp.arange(members) == member, page_counts, 0)) * PAGE
-    start = jnp.clip(part * length - before, -length, slot_rows)
-    padded = jnp.pad(cache_tiles, ((length, length), (0, 0)))
-    rows = lax.dynamic_slice(padded, (start + length, 0), (length, full))
-    index = start + jnp.arange(length)
-    mine = (index >= 0) & (index < count)
-    return jnp.where(mine[:, None], rows, jnp.zeros((), rows.dtype))
+    slots = slot_rows // PAGE
+    pages = slots * members // SLOTS_PER_LIVE // parts
+    before = jnp.sum(jnp.where(jnp.arange(members) < member, page_counts, 0))
+    count = jnp.sum(jnp.where(jnp.arange(members) == member, page_counts, 0))
+    place = jnp.stack([part * pages - before, count]).astype(jnp.int32)
+    return pl.pallas_call(
+        page_kernel,
+        grid_spec=pltpu.PrefetchScalarGridSpec(
+            num_scalar_prefetch=1,
+            grid=(pages,),
+            in_specs=[
+                pl.BlockSpec((PAGE, full), lambda i, place: (jnp.clip(place[0] + i, 0, slots - 1), 0))
+            ],
+            out_specs=pl.BlockSpec((PAGE, full), lambda i, place: (i, 0)),
+        ),
+        out_shape=jax.ShapeDtypeStruct((pages * PAGE, full), cache_tiles.dtype),
+    )(place, cache_tiles)
+
+
+def share_kernel(
+    members, parts, own_ref, keys_ref, up_ref, down_ref, up_out, down_out,
+    up_send, up_recv, down_send, down_recv, x_send, x_recv, core_send, core_recv,
+):
+    m = lax.axis_index("pages")
+    part = lax.axis_index("heads")
+    chips = parts // CORES
+    chip, core = part // CORES, part % CORES
+    sibling = chip * CORES + (CORES - 1 - core)
+    length = own_ref.shape[0]
+    chunks = length // PAGE
+    last = members - 1
+    has_low, has_high = m > 0, m < last
+
+    def across(k):
+        return lax.rem(chip + k, chips) * CORES + core
+
+    barrier = pltpu.get_barrier_semaphore()
+
+    @pl.when(has_low)
+    def _():
+        pl.semaphore_signal(barrier, inc=1, device_id={"pages": m - 1}, device_id_type=MESH)
+
+    @pl.when(has_high)
+    def _():
+        pl.semaphore_signal(barrier, inc=1, device_id={"pages": m + 1}, device_id_type=MESH)
+
+    for k in range(1, chips):
+        pl.semaphore_signal(barrier, inc=1, device_id={"heads": across(k)}, device_id_type=MESH)
+    pl.semaphore_signal(barrier, inc=1, device_id={"heads": sibling}, device_id_type=MESH)
+
+    @pl.when(m == 0)
+    def _():
+        up_ref[...] = jnp.zeros_like(up_ref)
+
+    @pl.when(m == last)
+    def _():
+        down_ref[...] = jnp.zeros_like(down_ref)
+
+    pl.semaphore_wait(barrier, chips + has_low.astype(jnp.int32) + has_high.astype(jnp.int32))
+
+    def rows(c):
+        return pl.ds(pl.multiple_of(c * PAGE, PAGE), PAGE)
+
+    def key_rows(p, c):
+        return pl.ds(pl.multiple_of(p * length + c * PAGE, PAGE), PAGE)
+
+    def up_copy(c):
+        return pltpu.make_async_remote_copy(
+            up_out.at[rows(c)], up_ref.at[rows(c)], up_send.at[c], up_recv.at[c],
+            device_id={"pages": m + 1}, device_id_type=MESH,
+        )
+
+    def down_copy(c):
+        return pltpu.make_async_remote_copy(
+            down_out.at[rows(c)], down_ref.at[rows(c)], down_send.at[c], down_recv.at[c],
+            device_id={"pages": m - 1}, device_id_type=MESH,
+        )
+
+    def x_copy(k, p, c):
+        return pltpu.make_async_remote_copy(
+            keys_ref.at[key_rows(p, c)], keys_ref.at[key_rows(p, c)],
+            x_send.at[k, c], x_recv.at[k, c],
+            device_id={"heads": across(k)}, device_id_type=MESH,
+        )
+
+    def core_copy(k, p, c):
+        return pltpu.make_async_remote_copy(
+            keys_ref.at[key_rows(p, c)], keys_ref.at[key_rows(p, c)],
+            core_send.at[k, c], core_recv.at[k, c],
+            device_id={"heads": sibling}, device_id_type=MESH,
+        )
+
+    late = jnp.maximum(m, last - m)
+
+    def step(t, _):
+        c_up = t - m
+        c_down = t - (last - m)
+        c_done = t - late
+        c_next = t - late - 1
+
+        @pl.when((c_up >= 0) & (c_up < chunks))
+        def _():
+            @pl.when(has_low)
+            def _():
+                up_copy(c_up).wait_recv()
+
+            @pl.when(has_high)
+            def _():
+                up_out[rows(c_up), :] = up_ref[rows(c_up), :] + own_ref[rows(c_up), :]
+                up_copy(c_up).start()
+
+        @pl.when((c_down >= 0) & (c_down < chunks))
+        def _():
+            @pl.when(has_high)
+            def _():
+                down_copy(c_down).wait_recv()
+
+            @pl.when(has_low)
+            def _():
+                down_out[rows(c_down), :] = down_ref[rows(c_down), :] + own_ref[rows(c_down), :]
+                down_copy(c_down).start()
+
+        @pl.when((c_done >= 0) & (c_done < chunks))
+        def _():
+            keys_ref[key_rows(part, c_done), :] = (
+                up_ref[rows(c_done), :] + own_ref[rows(c_done), :] + down_ref[rows(c_done), :]
+            )
+            for k in range(1, chips):
+                x_copy(k, part, c_done).start()
+            core_copy(0, part, c_done).start()
+
+        @pl.when((c_next >= 0) & (c_next < chunks))
+        def _():
+            for k in range(1, chips):
+                sender = lax.rem(chip + chips - k, chips) * CORES + core
+                x_copy(k, sender, c_next).wait_recv()
+                core_copy(k, sender, c_next).start()
+
+        return 0
+
+    lax.fori_loop(0, chunks + members, step, 0)
+
+    def finish(c, _):
+        @pl.when(has_high)
+        def _():
+            up_copy(c).wait_send()
+
+        @pl.when(has_low)
+        def _():
+            down_copy(c).wait_send()
+
+        for k in range(chips):
+            origin = lax.rem(chip + chips - k, chips) * CORES
+            if k:
+                x_copy(k, part, c).wait_send()
+            core_copy(k, origin + core, c).wait_send()
+            core_copy(k, origin + (CORES - 1 - core), c).wait_recv()
+        return 0
+
+    lax.fori_loop(0, chunks, finish, 0)
+
+
+def share(own, members, parts):
+    length, full = own.shape
+    chunks = length // PAGE
+    chips = parts // CORES
+    buffer = pltpu.VMEM((length, full), own.dtype)
+    line = pltpu.SemaphoreType.DMA((chunks,))
+    wide = pltpu.SemaphoreType.DMA((chips, chunks))
+    vmem = pl.BlockSpec(memory_space=pltpu.VMEM)
+    return pl.pallas_call(
+        functools.partial(share_kernel, members, parts),
+        out_shape=jax.ShapeDtypeStruct((parts * length, full), own.dtype),
+        in_specs=[vmem],
+        out_specs=vmem,
+        scratch_shapes=[buffer] * 4 + [line] * 4 + [wide] * 4,
+        compiler_params=pltpu.CompilerParams(
+            collective_id=0, has_side_effects=True, vmem_limit_bytes=40 * 2**20
+        ),
+    )(own)
 
 
 def on_device(
@@ -116,8 +294,7 @@
     rows = q_nope.shape[0]
     tokens = query_token.shape[0]
     own = own_part(cache_tiles, page_counts, members, parts)
-    merged = lax.psum(own, "pages")
-    keys = lax.all_gather(merged, "heads", axis=0, tiled=True)
+    keys = share(own, members, parts)
     my_token = lax.dynamic_slice(query_token, (member * rows,), (rows,))
     limits = jnp.sum(
         jnp.where(my_token[:, None] == jnp.arange(tokens)[None, :], query_offsets[None, :], 0),

time: 133 us -> 116 us (0.87)
  waiting for transfers between devices: 97 us -> 26.1 us
  Pallas kernels: 12.4 us -> 61.5 us
  local copies, waits for them, and re-layouts: 3.52 us -> 7.92 us
    pallas_call x0 -> x2, Pallas kernels: none -> 49.2 us  [the longest x1 43.5 us: share(): pl.pallas_call(functools.partial(share_kernel, members, parts), out_shape...]
    psum x1 -> x0, waiting for transfers between devices: 43.3 us -> none  [on_device(): merged = lax.psum(own, 'pages')]
    all_gather x1 -> x0, waiting for transfers between devices: 25.6 us -> none  [on_device(): keys = lax.all_gather(merged, 'heads', axis=0, tiled=True)]
    unnamed x5 -> x7, local copies, waits for them, and re-layouts: 2.75 us -> 6.49 us
    all_gather x1, waiting for transfers between devices: 28.1 us -> 26 us  [on_device(): gathered = lax.all_gather(out, 'pages', axis=0, tiled=True)]
  transfers between devices with their start and end apart: 3 -> 1, of which waited for: 3 -> 1; matrix products, arithmetic and copies ran while one was open for 1% -> 0% of each run, Pallas kernels for 0% -> 0%
where the time goes in v2:
time: 116 us; the launch traced here: 115 us
  Pallas kernels  61.5 us (53%)
  waiting for transfers between devices  26.1 us (22%)
  between operations  14.1 us (12%)
  local copies, waits for them, and re-layouts  7.92 us (7%)
  other arithmetic  3.44 us (3%)
  matrix products  2.25 us (2%)
    pallas_call x1, Pallas kernels, share(): pl.pallas_call(functools.partial(share_kernel, members, parts), out_shape...  43.5 us
    all_gather x1, waiting for transfers between devices, on_device(): gathered = lax.all_gather(out, 'pages', axis=0, tiled=True)  26 us
    pallas_call x1, Pallas kernels, attend(): pl.pallas_call(functools.partial(attend_kernel, factor), grid=(heads // b...  12.4 us
    unnamed x7, local copies, waits for them, and re-layouts  6.49 us
    pallas_call x1, Pallas kernels, own_part(): pl.pallas_call(page_kernel, grid_spec=pltpu.PrefetchScalarGridSpec(num_sc...  5.7 us
  transfers between devices with their start and end apart: 1, of which 1 were waited for; matrix products, arithmetic and copies ran while one was open for 0% of the time, Pallas kernels for 0%

profile of v2, /device:TPU:0, one launch (start us, length us, event | category | flops | bytes accessed | tf_op | source)
XLA Modules:
  0.0 115.3 jit_solution(10201819530214423066)
XLA Ops:
  6.5 0.0 all-gather.2.cloned.1.call-start
  6.5 1.3 %fusion.3 = (s32[]{:T(128)}, s32[]{:T(128)}) fusion(s32[4]{0:T(128)} %param.13, s32[]{:T(128)S(6)} %axis_index.27), kind=kLoop, calls=%fused_computation.8 | loop fusion | flops 22 | bytes 28 | tf_op jit(solution)/shard_map/reduce_sum | solution.py:101
  7.9 0.7 dynamic_slice.3
  8.6 0.8 select_reduce_fusion
  9.4 0.7 copy.12.limits_ref
  10.1 3.9 %copy.11.cache_ref = bf16[1536,576]{1,0:T(8,128)(2,1)} copy(bf16[1536,576]{0,1:T(8,128)(2,1)} %param.10) | data formatting | bytes 3538944 | tf_op args[2]
  14.7 1.3 %pad_add_fusion.place_ref = s32[2]{0:T(128)} fusion(s32[1]{0:T(128)} %bitcast.2, s32[1]{0:T(128)} %bitcast.1), kind=kLoop, calls=%fused_computation.10 | loop fusion | flops 2 | bytes 16 | tf_op jit(solution)/shard_map/stack | solution.py:103
  16.0 5.7 %shard_map.82.own_ref = bf16[512,576]{1,0:T(8,128)(2,1)} custom-call(s32[2]{0:T(128)} %pad_add_fusion.place_ref, bf16[1536,576]{1,0:T(8,128)(2,1)} %copy.11.cache_ref), custom_call_target="tpu_custom_call" | custom-call | tf_op jit(solution)/shard_map/pallas_call | solution.py:104
  21.7 0.0 copy-start.1
  21.7 1.1 copy-done.1
  22.7 43.5 %shard_map.83.keys_ref = bf16[2048,576]{1,0:T(8,128)(2,1)S(1)} custom-call(bf16[512,576]{1,0:T(8,128)(2,1)S(1)} %copy-done.1), custom_call_target="tpu_custom_call" | custom-call | tf_op jit(solution)/shard_map/pallas_call | solution.py:269
  66.2 0.0 copy-start
  66.2 1.5 %copy-done = bf16[2048,576]{1,0:T(8,128)(2,1)} copy-done((bf16[2048,576]{1,0:T(8,128)(2,1)}, bf16[2048,576]{1,0:T(8,128)(2,1)S(1)}, u32[]{:S(2)}) %copy-start) | copy-done | bytes 2359320
  67.7 0.0 copy-start.2
  67.7 12.4 %shard_map.84 = bf16[32,4096]{1,0:T(8,128)(2,1)} custom-call(s32[32,1]{1,0:T(8,128)} %copy.12.limits_ref, bf16[32,4096]{1,0:T(8,128)(2,1)} %nope_ref.1, bf16[32,2048]{1,0:T(8,128)(2,1)} %rope_ref.1, bf16[2048,576]{1,0:T(8,128)(2,1)} %copy-done, bf16[32,128,512]{2,1,0:T(8,128)(2,1)} %wk_ref.1, bf16[32,512,128]{2,1,0:T(8,128)(2,1)} %wv_ref.1), custom_call_target="tpu_custom_call" | custom-call | flops 4563402752 | bytes 10747904 | tf_op jit(solution)/shard_map/pallas_call | solution.py:67
  80.1 0.0 all-gather.2.cloned.1.call-update
  80.1 26.0 %all-gather.2.cloned.1.call-done = bf16[128,4096]{1,0:T(8,128)(2,1)} async-done(((bf16[32,4096]{1,0:T(8,128)(2,1)}), bf16[128,4096]{1,0:T(8,128)(2,1)}) %all-gather.2.cloned.1.call-update) | async-done | bytes 1048592 | tf_op jit(solution)/shard_map/all_gather | solution.py:305
  106.2 0.0 copy-done.2
  106.2 2.2 %convolution_convert_fusion = bf16[32,4096]{1,0:T(8,128)(2,1)} fusion(bf16[128,4096]{1,0:T(8,128)(2,1)} %all-gather.2.cloned.1.call-done, s32[128]{0:T(128)S(1)} %copy-done.2, s32[32]{0:T(128)S(1)} %iota_add_fusion), kind=kOutput, calls=%fused_computation | convolution fusion | flops 33689600 | bytes 1311360 | tf_op jit(solution)/shard_map/dot_general | solution.py:308
  (1 shorter events, 0.0 us)
Async XLA Ops:
  6.5 99.6 %all-gather.2.cloned.1.call-start = ((), (), s32[]{:S(2)}) async-start(), calls=%async_computation | async-start | bytes 1310720 | tf_op jit(solution)/shard_map/all_gather | solution.py:305
  21.7 1.1 copy-start.1
  66.2 1.5 %copy-start = (bf16[2048,576]{1,0:T(8,128)(2,1)}, bf16[2048,576]{1,0:T(8,128)(2,1)S(1)}, u32[]{:S(2)}) copy-start(bf16[2048,576]{1,0:T(8,128)(2,1)S(1)} %shard_map.83.keys_ref) | copy-start | bytes 7077892
  67.7 38.5 %copy-start.2 = (s32[128]{0:T(128)S(1)}, s32[128]{0:T(128)}, u32[]{:S(2)}) copy-start(s32[128]{0:T(128)} %param.14) | copy-start | bytes 1540
Sparse Core Ops, SparseCore 0:
  80.2 25.8 all-gather.1

commit v3 on v2

--- a/solution.py
+++ b/solution.py
@@ -12,6 +12,7 @@
 SLOTS_PER_LIVE = 3
 HEAD_BLOCK = 8
 CORES = 2
+CHUNK = 128
 MESH = pl.DeviceIdType.MESH
 NEG = -1e30
 
@@ -86,33 +87,45 @@
     )(limits, q_nope, q_rope, keys, absorb_keys, absorb_values)
 
 
-def page_kernel(place_ref, cache_ref, out_ref):
-    slot = place_ref[0] + pl.program_id(0)
-    live = (slot >= 0) & (slot < place_ref[1])
-    out_ref[...] = jnp.where(live, cache_ref[...], jnp.zeros_like(cache_ref))
+def page_kernel(members, parts, counts_ref, cache_ref, out_ref, sems):
+    member = lax.axis_index("pages")
+    slots = cache_ref.shape[0] // PAGE
+    pages = out_ref.shape[0] // PAGE
+    before = lax.fori_loop(0, member, lambda j, total: total + counts_ref[j], jnp.int32(0))
+    count = counts_ref[member]
+    first = lax.axis_index("heads") * pages - before
+
+    def page(j):
+        slot = jnp.clip(first + j, 0, slots - 1)
+        return pltpu.make_async_copy(
+            cache_ref.at[pl.ds(pl.multiple_of(slot * PAGE, PAGE), PAGE)],
+            out_ref.at[pl.ds(j * PAGE, PAGE)],
+            sems.at[j],
+        )
+
+    for j in range(pages):
+        page(j).start()
+    for j in range(pages):
+        page(j).wait()
+
+        @pl.when((first + j < 0) | (first + j >= count))
+        def _():
+            out_ref[pl.ds(j * PAGE, PAGE), :] = jnp.zeros((PAGE, out_ref.shape[1]), out_ref.dtype)
 
 
 def own_part(cache_tiles, page_counts, members, parts):
-    member = lax.axis_index("pages")
-    part = lax.axis_index("heads")
     slot_rows, full = cache_tiles.shape
-    slots = slot_rows // PAGE
-    pages = slots * members // SLOTS_PER_LIVE // parts
-    before = jnp.sum(jnp.where(jnp.arange(members) < member, page_counts, 0))
-    count = jnp.sum(jnp.where(jnp.arange(members) == member, page_counts, 0))
-    place = jnp.stack([part * pages - before, count]).astype(jnp.int32)
+    pages = slot_rows // PAGE * members // SLOTS_PER_LIVE // parts
     return pl.pallas_call(
-        page_kernel,
-        grid_spec=pltpu.PrefetchScalarGridSpec(
-            num_scalar_prefetch=1,
-            grid=(pages,),
-            in_specs=[
-                pl.BlockSpec((PAGE, full), lambda i, place: (jnp.clip(place[0] + i, 0, slots - 1), 0))
-            ],
-            out_specs=pl.BlockSpec((PAGE, full), lambda i, place: (i, 0)),
-        ),
+        functools.partial(page_kernel, members, parts),
+        in_specs=[
+            pl.BlockSpec(memory_space=pltpu.SMEM),
+            pl.BlockSpec(memory_space=pl.ANY),
+        ],
+        out_specs=pl.BlockSpec(memory_space=pltpu.VMEM),
         out_shape=jax.ShapeDtypeStruct((pages * PAGE, full), cache_tiles.dtype),
-    )(place, cache_tiles)
+        scratch_shapes=[pltpu.SemaphoreType.DMA((pages,))],
+    )(page_counts, cache_tiles)
 
 
 def share_kernel(
@@ -125,7 +138,7 @@
     chip, core = part // CORES, part % CORES
     sibling = chip * CORES + (CORES - 1 - core)
     length = own_ref.shape[0]
-    chunks = length // PAGE
+    chunks = length // CHUNK
     last = members - 1
     has_low, has_high = m > 0, m < last
 
@@ -157,10 +170,10 @@
     pl.semaphore_wait(barrier, chips + has_low.astype(jnp.int32) + has_high.astype(jnp.int32))
 
     def rows(c):
-        return pl.ds(pl.multiple_of(c * PAGE, PAGE), PAGE)
+        return pl.ds(pl.multiple_of(c * CHUNK, CHUNK), CHUNK)
 
     def key_rows(p, c):
-        return pl.ds(pl.multiple_of(p * length + c * PAGE, PAGE), PAGE)
+        return pl.ds(pl.multiple_of(p * length + c * CHUNK, CHUNK), CHUNK)
 
     def up_copy(c):
         return pltpu.make_async_remote_copy(
@@ -260,7 +273,7 @@
 
 def share(own, members, parts):
     length, full = own.shape
-    chunks = length // PAGE
+    chunks = length // CHUNK
     chips = parts // CORES
     buffer = pltpu.VMEM((length, full), own.dtype)
     line = pltpu.SemaphoreType.DMA((chunks,))

time: 116 us -> 105 us (0.905)
  Pallas kernels: 61.5 us -> 54.3 us
  other arithmetic: 3.44 us -> 0.84 us
    pallas_call x1, Pallas kernels: 43.5 us -> 39.1 us  [share(): pl.pallas_call(functools.partial(share_kernel, members, parts), out_shape...]
    pallas_call x1, Pallas kernels: 5.7 us -> 2.77 us  [own_part(): pl.pallas_call(functools.partial(page_kernel, members, parts), in_specs=[...]
    reduce_sum x1 -> x0, other arithmetic: 1.32 us -> none  [own_part(): before = jnp.sum(jnp.where(jnp.arange(members) < member, page_counts, 0))]
    another operation x1 -> x0, other arithmetic: 1.29 us -> none  [own_part(): place = jnp.stack([part * pages - before, count]).astype(jnp.int32)]
where the time goes in v3:
time: 105 us
  Pallas kernels  54.3 us (52%)
  waiting for transfers between devices  26.5 us (25%)
  between operations  13.4 us (13%)
  local copies, waits for them, and re-layouts  7.92 us (8%)
  matrix products  2.25 us (2%)
    pallas_call x1, Pallas kernels, share(): pl.pallas_call(functools.partial(share_kernel, members, parts), out_shape...  39.1 us
    all_gather x1, waiting for transfers between devices, on_device(): gathered = lax.all_gather(out, 'pages', axis=0, tiled=True)  26.5 us
    pallas_call x1, Pallas kernels, attend(): pl.pallas_call(functools.partial(attend_kernel, factor), grid=(heads // b...  12.4 us
    unnamed x7, local copies, waits for them, and re-layouts  6.5 us
    pallas_call x1, Pallas kernels, own_part(): pl.pallas_call(functools.partial(page_kernel, members, parts), in_specs=[...  2.77 us
    dot_general x1, matrix products, on_device(): jnp.dot(pick, gathered, preferred_element_type=jnp.float32)  2.25 us
  transfers between devices with their start and end apart: 1, of which 1 were waited for; matrix products, arithmetic and copies ran while one was open for 0% of the time, Pallas kernels for 0%

profile of v3, /device:TPU:0, one launch (start us, length us, event | category | flops | bytes accessed | tf_op | source)
XLA Modules:
  0.0 105.2 jit_solution(4217097609811897168)
XLA Ops:
  6.5 0.0 all-gather.2.cloned.1.call-start
  6.5 0.7 dynamic_slice.3
  7.3 0.8 select_reduce_fusion
  8.1 0.7 copy.12.limits_ref
  8.8 3.9 %copy.11.cache_ref = bf16[1536,576]{1,0:T(8,128)(2,1)} copy(bf16[1536,576]{0,1:T(8,128)(2,1)} %param.10) | data formatting | bytes 3538944 | tf_op args[2]
  12.7 2.8 %shard_map.82.own_ref = bf16[512,576]{1,0:T(8,128)(2,1)} custom-call(s32[4]{0:T(128)} %counts_ref.1, bf16[1536,576]{1,0:T(8,128)(2,1)} %copy.11.cache_ref), custom_call_target="tpu_custom_call" | custom-call | tf_op jit(solution)/shard_map/pallas_call | solution.py:119
  15.5 0.0 copy-start.1
  15.5 1.1 %copy-done.1 = bf16[512,576]{1,0:T(8,128)(2,1)S(1)} copy-done((bf16[512,576]{1,0:T(8,128)(2,1)S(1)}, bf16[512,576]{1,0:T(8,128)(2,1)}, u32[]{:S(2)}) %copy-start.1) | copy-done | bytes 589848
  16.6 39.1 %shard_map.83.keys_ref = bf16[2048,576]{1,0:T(8,128)(2,1)S(1)} custom-call(bf16[512,576]{1,0:T(8,128)(2,1)S(1)} %copy-done.1), custom_call_target="tpu_custom_call" | custom-call | tf_op jit(solution)/shard_map/pallas_call | solution.py:282
  55.7 0.0 copy-start
  55.7 1.5 %copy-done = bf16[2048,576]{1,0:T(8,128)(2,1)} copy-done((bf16[2048,576]{1,0:T(8,128)(2,1)}, bf16[2048,576]{1,0:T(8,128)(2,1)S(1)}, u32[]{:S(2)}) %copy-start) | copy-done | bytes 2359320
  57.2 0.0 copy-start.2
  57.2 12.4 %shard_map.84 = bf16[32,4096]{1,0:T(8,128)(2,1)} custom-call(s32[32,1]{1,0:T(8,128)} %copy.12.limits_ref, bf16[32,4096]{1,0:T(8,128)(2,1)} %nope_ref.1, bf16[32,2048]{1,0:T(8,128)(2,1)} %rope_ref.1, bf16[2048,576]{1,0:T(8,128)(2,1)} %copy-done, bf16[32,128,512]{2,1,0:T(8,128)(2,1)} %wk_ref.1, bf16[32,512,128]{2,1,0:T(8,128)(2,1)} %wv_ref.1), custom_call_target="tpu_custom_call" | custom-call | flops 4563402752 | bytes 10747904 | tf_op jit(solution)/shard_map/pallas_call | solution.py:68
  69.6 0.0 all-gather.2.cloned.1.call-update
  69.6 26.5 %all-gather.2.cloned.1.call-done = bf16[128,4096]{1,0:T(8,128)(2,1)} async-done(((bf16[32,4096]{1,0:T(8,128)(2,1)}), bf16[128,4096]{1,0:T(8,128)(2,1)}) %all-gather.2.cloned.1.call-update) | async-done | bytes 1048592 | tf_op jit(solution)/shard_map/all_gather | solution.py:318
  96.1 0.0 copy-done.2
  96.2 2.2 %convolution_convert_fusion = bf16[32,4096]{1,0:T(8,128)(2,1)} fusion(bf16[128,4096]{1,0:T(8,128)(2,1)} %all-gather.2.cloned.1.call-done, s32[128]{0:T(128)S(1)} %copy-done.2, s32[32]{0:T(128)S(1)} %iota_add_fusion), kind=kOutput, calls=%fused_computation | convolution fusion | flops 33689600 | bytes 1311360 | tf_op jit(solution)/shard_map/dot_general | solution.py:321
  (1 shorter events, 0.0 us)
Async XLA Ops:
  6.5 89.6 %all-gather.2.cloned.1.call-start = ((), (), s32[]{:S(2)}) async-start(), calls=%async_computation | async-start | bytes 1310720 | tf_op jit(solution)/shard_map/all_gather | solution.py:318
  15.5 1.1 %copy-start.1 = (bf16[512,576]{1,0:T(8,128)(2,1)S(1)}, bf16[512,576]{1,0:T(8,128)(2,1)}, u32[]{:S(2)}) copy-start(bf16[512,576]{1,0:T(8,128)(2,1)} %shard_map.82.own_ref) | copy-start | bytes 1769476
  55.7 1.5 %copy-start = (bf16[2048,576]{1,0:T(8,128)(2,1)}, bf16[2048,576]{1,0:T(8,128)(2,1)S(1)}, u32[]{:S(2)}) copy-start(bf16[2048,576]{1,0:T(8,128)(2,1)S(1)} %shard_map.83.keys_ref) | copy-start | bytes 7077892
  57.2 38.9 %copy-start.2 = (s32[128]{0:T(128)S(1)}, s32[128]{0:T(128)}, u32[]{:S(2)}) copy-start(s32[128]{0:T(128)} %param.14) | copy-start | bytes 1540
Sparse Core Ops, SparseCore 0:
  69.8 26.3 all-gather.1

commit v4 on v3

--- a/solution.py
+++ b/solution.py
@@ -17,7 +17,25 @@
 NEG = -1e30
 
 
-def attend_kernel(factor, limits_ref, nope_ref, rope_ref, keys_ref, wk_ref, wv_ref, out_ref):
+def attend_kernel(
+    factor, members, blocks, limits_ref, token_ref, nope_ref, rope_ref, keys_ref, wk_ref, wv_ref, out_ref,
+    held, up_send, up_recv, down_send, down_recv,
+):
+    m = lax.axis_index("pages")
+    last = members - 1
+    now = pl.program_id(0)
+
+    @pl.when(now == 0)
+    def _():
+        barrier = pltpu.get_barrier_semaphore()
+        for there, step in ((m > 0, -1), (m < last, 1)):
+
+            @pl.when(there)
+            def _(step=step):
+                pl.semaphore_signal(barrier, inc=1, device_id={"pages": m + step}, device_id_type=MESH)
+
+        pl.semaphore_wait(barrier, (m > 0).astype(jnp.int32) + (m < last).astype(jnp.int32))
+
     block, nope_width, latent = wk_ref.shape
     rows = nope_ref.shape[0]
     value_width = wv_ref.shape[2]
@@ -51,13 +69,70 @@
         weights.astype(jnp.bfloat16), keys_ref[:, :latent], preferred_element_type=jnp.float32
     )
     mixed = (mixed / total).astype(jnp.bfloat16)
+    mine = pl.ds(pl.multiple_of(m * rows, rows), rows)
     for h in range(block):
-        out_ref[:, h * value_width : (h + 1) * value_width] = jnp.dot(
+        held[now, mine, h * value_width : (h + 1) * value_width] = jnp.dot(
             mixed[h * rows : (h + 1) * rows], wv_ref[h], preferred_element_type=jnp.float32
-        ).astype(out_ref.dtype)
-
-
-def attend(limits, q_nope, q_rope, keys, absorb_keys, absorb_values):
+        ).astype(held.dtype)
+
+    def hop(origin, d, b, step, send, recv):
+        part = held.at[b, pl.ds(pl.multiple_of(origin * rows, rows), rows)]
+        return pltpu.make_async_remote_copy(
+            part, part, send.at[d, b], recv.at[d, b],
+            device_id={"pages": m + step}, device_id_type=MESH,
+        )
+
+    ways = ((1, up_send, up_recv), (-1, down_send, down_recv))
+
+    def tick(t):
+        def distance(d, _):
+            b = t - d
+            for step, send, recv in ways:
+                origin = m - step * d
+                there = (b >= 0) & (b < blocks) & (origin >= 0) & (origin <= last)
+
+                @pl.when(there & (d > 0))
+                def _(step=step, send=send, recv=recv, origin=origin):
+                    hop(origin, d - 1, b, step, send, recv).wait_recv()
+
+                @pl.when(there & (m + step >= 0) & (m + step <= last))
+                def _(step=step, send=send, recv=recv, origin=origin):
+                    hop(origin, d, b, step, send, recv).start()
+
+            return 0
+
+        lax.fori_loop(0, members, distance, 0)
+
+    tick(now)
+
+    @pl.when(now == blocks - 1)
+    def _():
+        lax.fori_loop(blocks, blocks + last, lambda t, _: (tick(t), 0)[1], 0)
+
+        def sent(i, _):
+            d, b = i // blocks, i % blocks
+            for step, send, recv in ways:
+                origin = m - step * d
+                there = (origin >= 0) & (origin <= last) & (m + step >= 0) & (m + step <= last)
+
+                @pl.when(there)
+                def _(step=step, send=send, recv=recv, origin=origin):
+                    hop(origin, d, b, step, send, recv).wait_send()
+
+            return 0
+
+        lax.fori_loop(0, members * blocks, sent, 0)
+        tokens = held.shape[1]
+        wanted = m * rows + lax.broadcasted_iota(jnp.int32, (rows, tokens), 0)
+        pick = (wanted == token_ref[...]).astype(jnp.bfloat16)
+        wide = block * value_width
+        for b in range(blocks):
+            out_ref[:, b * wide : (b + 1) * wide] = jnp.dot(
+                pick, held[b], preferred_element_type=jnp.float32
+            ).astype(out_ref.dtype)
+
+
+def attend(members, limits, query_token, q_nope, q_rope, keys, absorb_keys, absorb_values):
     heads, nope_width, latent = absorb_keys.shape
     value_width = absorb_values.shape[2]
     rows = q_nope.shape[0]
@@ -66,25 +141,32 @@
     factor = (nope_width + rope_width) ** (-0.5) * math.log2(math.e)
     live, full = keys.shape
     return pl.pallas_call(
-        functools.partial(attend_kernel, factor),
+        functools.partial(attend_kernel, factor, members, heads // block),
         grid=(heads // block,),
         out_shape=jax.ShapeDtypeStruct((rows, heads * value_width), jnp.bfloat16),
         in_specs=[
             pl.BlockSpec((rows, 1), lambda i: (0, 0)),
+            pl.BlockSpec((1, members * rows), lambda i: (0, 0)),
             pl.BlockSpec((rows, block * nope_width), lambda i: (0, i)),
             pl.BlockSpec((rows, block * rope_width), lambda i: (0, i)),
             pl.BlockSpec((live, full), lambda i: (0, 0)),
             pl.BlockSpec((block, nope_width, latent), lambda i: (i, 0, 0)),
             pl.BlockSpec((block, latent, value_width), lambda i: (i, 0, 0)),
         ],
-        out_specs=pl.BlockSpec((rows, block * value_width), lambda i: (0, i)),
-        compiler_params=pltpu.CompilerParams(vmem_limit_bytes=56 * 2**20),
+        out_specs=pl.BlockSpec((rows, heads * value_width), lambda i: (0, 0)),
+        scratch_shapes=[
+            pltpu.VMEM((heads // block, members * rows, block * value_width), jnp.bfloat16)
+        ]
+        + [pltpu.SemaphoreType.DMA((members, heads // block))] * 4,
+        compiler_params=pltpu.CompilerParams(
+            collective_id=1, has_side_effects=True, vmem_limit_bytes=56 * 2**20
+        ),
         cost_estimate=pl.CostEstimate(
             flops=2 * rows * heads * live * (full + latent),
             bytes_accessed=2 * (absorb_keys.size + absorb_values.size + keys.size),
             transcendentals=rows * heads * live,
         ),
-    )(limits, q_nope, q_rope, keys, absorb_keys, absorb_values)
+    )(limits, query_token[None, :], q_nope, q_rope, keys, absorb_keys, absorb_values)
 
 
 def page_kernel(members, parts, counts_ref, cache_ref, out_ref, sems):
@@ -314,11 +396,9 @@
         axis=1,
         keepdims=True,
     )
-    out = attend(limits, q_nope, q_rope, keys, absorb_keys, absorb_values)
-    gathered = lax.all_gather(out, "pages", axis=0, tiled=True)
-    wanted = member * rows + jnp.arange(rows)
-    pick = (wanted[:, None] == query_token[None, :]).astype(jnp.bfloat16)
-    return jnp.dot(pick, gathered, preferred_element_type=jnp.float32).astype(jnp.bfloat16)
+    return attend(
+        members, limits, query_token, q_nope, q_rope, keys, absorb_keys, absorb_values
+    )
 
 
 def solution(mesh):

time: 105 us -> 80.3 us (0.76)
  waiting for transfers between devices: 26.5 us -> 0 us
  Pallas kernels: 54.3 us -> 69.5 us
  between operations: 13.4 us -> 0.04 us
  matrix products: 2.25 us -> 0 us
  local copies, waits for them, and re-layouts: 7.92 us -> 9.58 us
    all_gather x1 -> x0, waiting for transfers between devices: 26.5 us -> none  [on_device(): gathered = lax.all_gather(out, 'pages', axis=0, tiled=True)]
    pallas_call x1, Pallas kernels: 12.4 us -> 27.2 us  [attend(): pl.pallas_call(functools.partial(attend_kernel, factor, members, heads //...]
    dot_general x1 -> x0, matrix products: 2.25 us -> none  [on_device(): jnp.dot(pick, gathered, preferred_element_type=jnp.float32)]
    unnamed x7 -> x6, local copies, waits for them, and re-layouts: 6.5 us -> 8.15 us
  transfers between devices with their start and end apart: 1 -> 0, of which waited for: 1 -> 0; matrix products, arithmetic and copies ran while one was open for 0% -> 0% of each run, Pallas kernels for 0% -> 0%
where the time goes in v4:
time: 80.3 us; the launch traced here: 79.9 us
  Pallas kernels  69.5 us (87%)
  local copies, waits for them, and re-layouts  9.58 us (12%)
  other arithmetic  0.83 us (1%)
    pallas_call x1, Pallas kernels, share(): pl.pallas_call(functools.partial(share_kernel, members, parts), out_shape...  39.5 us
    pallas_call x1, Pallas kernels, attend(): pl.pallas_call(functools.partial(attend_kernel, factor, members, heads //...  27.2 us
    unnamed x6, local copies, waits for them, and re-layouts  8.15 us
    pallas_call x1, Pallas kernels, own_part(): pl.pallas_call(functools.partial(page_kernel, members, parts), in_specs=[...  2.77 us

profile of v4, /device:TPU:0, one launch (start us, length us, event | category | flops | bytes accessed | tf_op | source)
XLA Modules:
  0.0 79.9 jit_solution(17006680843899008329)
XLA Ops:
  0.0 0.7 dynamic_slice.3
  0.7 0.8 %select_reduce_fusion = s32[32]{0:T(128)S(1)} fusion(s32[128]{0:T(128)} %param.15, s32[32]{0:T(128)S(1)} %dynamic_slice.3), kind=kLoop, calls=%fused_computation | loop fusion | flops 12256 | bytes 768 | tf_op jit(solution)/shard_map/reduce_sum | solution.py:394
  1.6 0.7 copy.12.limits_ref
  2.3 3.9 %copy.11.cache_ref = bf16[1536,576]{1,0:T(8,128)(2,1)} copy(bf16[1536,576]{0,1:T(8,128)(2,1)} %param.10) | data formatting | bytes 3538944 | tf_op args[2]
  6.2 2.8 %shard_map.82.own_ref = bf16[512,576]{1,0:T(8,128)(2,1)} custom-call(s32[4]{0:T(128)} %counts_ref.1, bf16[1536,576]{1,0:T(8,128)(2,1)} %copy.11.cache_ref), custom_call_target="tpu_custom_call" | custom-call | tf_op jit(solution)/shard_map/pallas_call | solution.py:201
  9.0 0.0 copy-start.1
  9.0 1.1 %copy-done.1 = bf16[512,576]{1,0:T(8,128)(2,1)S(1)} copy-done((bf16[512,576]{1,0:T(8,128)(2,1)S(1)}, bf16[512,576]{1,0:T(8,128)(2,1)}, u32[]{:S(2)}) %copy-start.1) | copy-done | bytes 589848
  10.0 39.5 %shard_map.83.keys_ref = bf16[2048,576]{1,0:T(8,128)(2,1)S(1)} custom-call(bf16[512,576]{1,0:T(8,128)(2,1)S(1)} %copy-done.1), custom_call_target="tpu_custom_call" | custom-call | tf_op jit(solution)/shard_map/pallas_call | solution.py:364
  49.5 0.0 copy-start
  49.5 1.5 %copy-done = bf16[2048,576]{1,0:T(8,128)(2,1)} copy-done((bf16[2048,576]{1,0:T(8,128)(2,1)}, bf16[2048,576]{1,0:T(8,128)(2,1)S(1)}, u32[]{:S(2)}) %copy-start) | copy-done | bytes 2359320
  51.0 27.2 %shard_map.84 = bf16[32,4096]{1,0:T(8,128)(2,1)} custom-call(s32[32,1]{1,0:T(8,128)} %copy.12.limits_ref, s32[1,128]{1,0:T(1,128)} %bitcast.3, bf16[32,4096]{1,0:T(8,128)(2,1)} %nope_ref.1, bf16[32,2048]{1,0:T(8,128)(2,1)} %rope_ref.1, bf16[2048,576]{1,0:T(8,128)(2,1)} %copy-done, bf16[32,128,512]{2,1,0:T(8,128)(2,1)} %wk_ref.1, bf16[32,512,128]{2,1,0:T(8,128)(2,1)} %wv_ref.1), custom_call_target="tpu_custom_call" | custom-call | flops 4563402752 | bytes 10747904 | tf_op jit(solution)/shard_map/pallas_call | solution.py:143
  78.3 1.7 %copy.14 = bf16[32,4096]{1,0:T(8,128)(2,1)} copy(bf16[32,4096]{1,0:T(8,128)(2,1)} %shard_map.84) | data formatting | bytes 524288
Async XLA Ops:
  9.0 1.1 %copy-start.1 = (bf16[512,576]{1,0:T(8,128)(2,1)S(1)}, bf16[512,576]{1,0:T(8,128)(2,1)}, u32[]{:S(2)}) copy-start(bf16[512,576]{1,0:T(8,128)(2,1)} %shard_map.82.own_ref) | copy-start | bytes 1769476
  49.5 1.5 %copy-start = (bf16[2048,576]{1,0:T(8,128)(2,1)}, bf16[2048,576]{1,0:T(8,128)(2,1)S(1)}, u32[]{:S(2)}) copy-start(bf16[2048,576]{1,0:T(8,128)(2,1)S(1)} %shard_map.83.keys_ref) | copy-start | bytes 7077892

commit v5 on v4

--- a/solution.py
+++ b/solution.py
@@ -18,7 +18,7 @@
 
 
 def attend_kernel(
-    factor, members, blocks, limits_ref, token_ref, nope_ref, rope_ref, keys_ref, wk_ref, wv_ref, out_ref,
+    factor, members, blocks, offset_ref, token_ref, nope_ref, rope_ref, keys_ref, wk_ref, wv_ref, out_ref,
     held, up_send, up_recv, down_send, down_recv,
 ):
     m = lax.axis_index("pages")
@@ -59,7 +59,18 @@
     ) + lax.dot_general(
         q_rope, keys_ref[:, latent:], contract, preferred_element_type=jnp.float32
     )
-    limits = jnp.concatenate([limits_ref[...]] * block, axis=0)
+    square = (rows, token_ref.shape[1])
+    lane = lax.broadcasted_iota(jnp.int32, square, 1)
+    here = lane == m * rows + lax.broadcasted_iota(jnp.int32, square, 0)
+    token = jnp.sum(
+        jnp.where(here, token_ref[...].astype(jnp.float32), 0.0), axis=1, keepdims=True
+    )
+    limit = jnp.sum(
+        jnp.where(lane.astype(jnp.float32) == token, offset_ref[...].astype(jnp.float32), 0.0),
+        axis=1,
+        keepdims=True,
+    ).astype(jnp.int32)
+    limits = jnp.concatenate([limit] * block, axis=0)
     position = lax.broadcasted_iota(jnp.int32, scores.shape, 1)
     scores = jnp.where(position < limits, scores, NEG)
     top = jnp.max(scores, axis=1, keepdims=True)
@@ -132,7 +143,7 @@
             ).astype(out_ref.dtype)
 
 
-def attend(members, limits, query_token, q_nope, q_rope, keys, absorb_keys, absorb_values):
+def attend(members, query_offsets, query_token, q_nope, q_rope, keys, absorb_keys, absorb_values):
     heads, nope_width, latent = absorb_keys.shape
     value_width = absorb_values.shape[2]
     rows = q_nope.shape[0]
@@ -145,7 +156,7 @@
         grid=(heads // block,),
         out_shape=jax.ShapeDtypeStruct((rows, heads * value_width), jnp.bfloat16),
         in_specs=[
-            pl.BlockSpec((rows, 1), lambda i: (0, 0)),
+            pl.BlockSpec((1, members * rows), lambda i: (0, 0)),
             pl.BlockSpec((1, members * rows), lambda i: (0, 0)),
             pl.BlockSpec((rows, block * nope_width), lambda i: (0, i)),
             pl.BlockSpec((rows, block * rope_width), lambda i: (0, i)),
@@ -166,7 +177,7 @@
             bytes_accessed=2 * (absorb_keys.size + absorb_values.size + keys.size),
             transcendentals=rows * heads * live,
         ),
-    )(limits, query_token[None, :], q_nope, q_rope, keys, absorb_keys, absorb_values)
+    )(query_offsets[None, :], query_token[None, :], q_nope, q_rope, keys, absorb_keys, absorb_values)
 
 
 def page_kernel(members, parts, counts_ref, cache_ref, out_ref, sems):
@@ -385,19 +396,10 @@
     query_token,
     query_offsets,
 ):
-    member = lax.axis_index("pages")
-    rows = q_nope.shape[0]
-    tokens = query_token.shape[0]
     own = own_part(cache_tiles, page_counts, members, parts)
     keys = share(own, members, parts)
-    my_token = lax.dynamic_slice(query_token, (member * rows,), (rows,))
-    limits = jnp.sum(
-        jnp.where(my_token[:, None] == jnp.arange(tokens)[None, :], query_offsets[None, :], 0),
-        axis=1,
-        keepdims=True,
-    )
     return attend(
-        members, limits, query_token, q_nope, q_rope, keys, absorb_keys, absorb_values
+        members, query_offsets, query_token, q_nope, q_rope, keys, absorb_keys, absorb_values
     )
 
 

time: 80.3 us -> 78.3 us (0.975)
  local copies, waits for them, and re-layouts: 9.58 us -> 8.17 us
  other arithmetic: 0.83 us -> 0 us
    reduce_sum x1 -> x0, other arithmetic: 0.83 us -> none  [on_device(): jnp.sum(jnp.where(my_token[:, None] == jnp.arange(tokens)[None, :], query...]
where the time goes in v5:
time: 78.3 us
  Pallas kernels  70.1 us (90%)
  local copies, waits for them, and re-layouts  8.17 us (10%)
    pallas_call x1, Pallas kernels, share(): pl.pallas_call(functools.partial(share_kernel, members, parts), out_shape...  40.1 us
    pallas_call x1, Pallas kernels, attend(): pl.pallas_call(functools.partial(attend_kernel, factor, members, heads //...  27.3 us
    unnamed x6, local copies, waits for them, and re-layouts  8.17 us
    pallas_call x1, Pallas kernels, own_part(): pl.pallas_call(functools.partial(page_kernel, members, parts), in_specs=[...  2.76 us

profile of v5, /device:TPU:0, one launch (start us, length us, event | category | flops | bytes accessed | tf_op | source)
XLA Modules:
  0.0 78.3 jit_solution(10765527115354912448)
XLA Ops:
  0.0 3.9 %copy.9.cache_ref = bf16[1536,576]{1,0:T(8,128)(2,1)} copy(bf16[1536,576]{0,1:T(8,128)(2,1)} %param.10) | data formatting | bytes 3538944 | tf_op args[2]
  3.9 2.8 %shard_map.82.own_ref = bf16[512,576]{1,0:T(8,128)(2,1)} custom-call(s32[4]{0:T(128)} %counts_ref.1, bf16[1536,576]{1,0:T(8,128)(2,1)} %copy.9.cache_ref), custom_call_target="tpu_custom_call" | custom-call | tf_op jit(solution)/shard_map/pallas_call | solution.py:212
  6.7 0.0 copy-start.1
  6.7 1.1 %copy-done.1 = bf16[512,576]{1,0:T(8,128)(2,1)S(1)} copy-done((bf16[512,576]{1,0:T(8,128)(2,1)S(1)}, bf16[512,576]{1,0:T(8,128)(2,1)}, u32[]{:S(2)}) %copy-start.1) | copy-done | bytes 589848
  7.8 40.1 %shard_map.83.keys_ref = bf16[2048,576]{1,0:T(8,128)(2,1)S(1)} custom-call(bf16[512,576]{1,0:T(8,128)(2,1)S(1)} %copy-done.1), custom_call_target="tpu_custom_call" | custom-call | tf_op jit(solution)/shard_map/pallas_call | solution.py:375
  47.8 0.0 copy-start
  47.8 1.5 %copy-done = bf16[2048,576]{1,0:T(8,128)(2,1)} copy-done((bf16[2048,576]{1,0:T(8,128)(2,1)}, bf16[2048,576]{1,0:T(8,128)(2,1)S(1)}, u32[]{:S(2)}) %copy-start) | copy-done | bytes 2359320
  49.3 27.3 %shard_map.84 = bf16[32,4096]{1,0:T(8,128)(2,1)} custom-call(s32[1,128]{1,0:T(1,128)} %bitcast.2, s32[1,128]{1,0:T(1,128)} %bitcast.3, bf16[32,4096]{1,0:T(8,128)(2,1)} %nope_ref.1, bf16[32,2048]{1,0:T(8,128)(2,1)} %rope_ref.1, bf16[2048,576]{1,0:T(8,128)(2,1)} %copy-done, bf16[32,128,512]{2,1,0:T(8,128)(2,1)} %wk_ref.1, bf16[32,512,128]{2,1,0:T(8,128)(2,1)} %wv_ref.1), custom_call_target="tpu_custom_call" | custom-call | flops 4563402752 | bytes 10747904 | tf_op jit(solution)/shard_map/pallas_call | solution.py:154
  76.6 1.7 %copy.11 = bf16[32,4096]{1,0:T(8,128)(2,1)} copy(bf16[32,4096]{1,0:T(8,128)(2,1)} %shard_map.84) | data formatting | bytes 524288
Async XLA Ops:
  6.7 1.1 %copy-start.1 = (bf16[512,576]{1,0:T(8,128)(2,1)S(1)}, bf16[512,576]{1,0:T(8,128)(2,1)}, u32[]{:S(2)}) copy-start(bf16[512,576]{1,0:T(8,128)(2,1)} %shard_map.82.own_ref) | copy-start | bytes 1769476
  47.8 1.5 %copy-start = (bf16[2048,576]{1,0:T(8,128)(2,1)}, bf16[2048,576]{1,0:T(8,128)(2,1)S(1)}, u32[]{:S(2)}) copy-start(bf16[2048,576]{1,0:T(8,128)(2,1)S(1)} %shard_map.83.keys_ref) | copy-start | bytes 7077892
